TPU v7x, 512 devices: a whole 4x4x16 slice. The times are simulated.
512 devices in a mesh: space: 128 (over z, x, core), basis: 4 (over y).
Axes of the slice: x: 4, y: 4, z: 16, core: 2. Of those that a mesh axis runs over, the one named last changes fastest.
Arguments:
- x_block: float32 [16, 3, 128, 32, 128], P(None, None, 'space', 'basis'), may hold values from -68 to 68
- basis: float32 [64, 3, 128, 32, 128], P('basis', None, 'space'), may hold values from -11 to 11
- material: int32 [128, 32, 128], P('space', 'basis'), may hold values from 0 to 7
- k0_blocks: float32 [8, 7, 3, 3], replicated, may hold values from -4 to 4
- k0_diag: float32 [8, 3], replicated, may hold values from 2 to 8
- ke_blocks: float32 [8, 7, 3, 3], replicated, may hold values from -6 to 6
- mass: float32 [8, 3], replicated, may hold values from 0.5 to 2
- velocities: float32 [1024], replicated, may hold values from 0.5 to 1
- shifts: float32 [1024], replicated, may hold values from 0.5 to 1.5
- sample: int32 [1], replicated, may hold values from 0 to 1023
Outputs:
- orthonormal: float32 [16, 3, 128, 32, 128], P(None, None, 'space', 'basis')
- coefficients: float32 [64, 16], P('basis')
- upper_factor: float32 [16, 16], replicated
All inputs are finite; a program needn't handle non-finite values.
Results may differ from a plain program's by a relative error of at most 0.00015.
Values sent between devices are 32-bit elements; how exact they have to be, the bound alone decides.
A program may use at most 64 MiB of HBM per device.

v0:
```python
import jax
import jax.numpy as jnp
from jax import lax
from jax.sharding import PartitionSpec as P

exact_precision = lax.Precision.HIGHEST


def with_halo(cells, sides, width):
    for axis, dim in sides:
        count = lax.axis_size(axis)
        ends = count - 1
        head = lax.slice_in_dim(cells, 0, width, axis=dim)
        tail = lax.slice_in_dim(cells, cells.shape[dim] - width, cells.shape[dim], axis=dim)
        cells = jnp.concatenate(
            [
                lax.ppermute(tail, axis, [(i, (i + 1) % count) for i in range(ends)]),
                cells,
                lax.ppermute(head, axis, [((i + 1) % count, i) for i in range(ends)]),
            ],
            axis=dim,
        )
    return cells


def stencil_tables(k0_blocks, k0_diag, ke_blocks, mass, velocities, shifts, sample):
    velocity = jnp.take(velocities, sample, axis=0)[0]
    sigma_value = jnp.take(shifts, sample, axis=0)[0]
    center = (k0_diag - sigma_value * mass)[:, :, None] * jnp.eye(3, dtype=jnp.float32)
    tables = k0_blocks - velocity * velocity * ke_blocks
    return tables.at[:, 0].add(center)


def neighbour_views(rimmed):
    centre = rimmed[:, :, 1:-1, 1:-1, :]
    lower_x = rimmed[:, :, :-2, 1:-1, :]
    upper_x = rimmed[:, :, 2:, 1:-1, :]
    lower_y = rimmed[:, :, 1:-1, :-2, :]
    upper_y = rimmed[:, :, 1:-1, 2:, :]
    zero_col = jnp.zeros(centre.shape[:4] + (1,), centre.dtype)
    lower_z = jnp.concatenate((zero_col, centre[:, :, :, :, :-1]), axis=4)
    upper_z = jnp.concatenate((centre[:, :, :, :, 1:], zero_col), axis=4)
    return [centre, lower_x, upper_x, lower_y, upper_y, lower_z, upper_z]


def cell_fields(tables, material_cells):
    material_count = tables.shape[0]
    fields = jnp.zeros((7, 3, 3) + material_cells.shape, jnp.float32)
    for level in range(material_count):
        chosen = (material_cells == level).astype(jnp.float32)
        fields = fields + tables[level][:, :, :, None, None, None] * chosen[None, None, None]
    return fields


def apply_fields(rimmed, fields):
    stencil_views = neighbour_views(rimmed)
    sums = [None, None, None]
    for offset in range(7):
        view = stencil_views[offset]
        for row in range(3):
            term = fields[offset, row, 0][None] * view[:, 0]
            term = term + fields[offset, row, 1][None] * view[:, 1]
            term = term + fields[offset, row, 2][None] * view[:, 2]
            sums[row] = term if sums[row] is None else sums[row] + term
    return jnp.stack(sums, axis=1)


def fine_image(x_block, material, tables):
    rimmed = with_halo(x_block, (("space", 2), ("basis", 3)), 1)
    return apply_fields(rimmed, cell_fields(tables, material))


def group_sum(partial_value):
    return lax.psum(partial_value, "space")


def scaled_block(fine_block, gram_matrix):
    block_cols = fine_block.shape[0]
    lower_factor = jnp.linalg.cholesky(gram_matrix)
    inverse = jax.scipy.linalg.solve_triangular(
        lower_factor, jnp.eye(block_cols, dtype=jnp.float32), lower=True
    ).T
    orthonormal = jnp.einsum("mcxyz,mn->ncxyz", fine_block, inverse, precision=exact_precision)
    return (orthonormal, lower_factor.T)


def finish(fine_block, row_count):
    gram_partial = jnp.einsum("ncxyz,mcxyz->nm", fine_block, fine_block, precision=exact_precision)
    gram_matrix = lax.psum(gram_partial, ("space", "basis")) / row_count
    return scaled_block(fine_block, gram_matrix)


def shards(
    x_block, basis, material, k0_blocks, k0_diag, ke_blocks, mass, velocities, shifts, sample
):
    tables = stencil_tables(k0_blocks, k0_diag, ke_blocks, mass, velocities, shifts, sample)
    block_cols = x_block.shape[0]
    extent_x = x_block.shape[2]
    extent_z = x_block.shape[4]
    full_y = basis.shape[3]
    group_cols = basis.shape[0]
    row_count = 3.0 * extent_x * lax.axis_size("space") * full_y * extent_z
    running = jnp.zeros((group_cols, block_cols), jnp.float32)
    fine_block = fine_image(x_block, material, tables)
    for repeat in range(2):
        partial_value = jnp.einsum(
            "kcxyz,ncxyz->kn",
            basis,
            lax.all_gather(fine_block, "basis", axis=3, tiled=True),
            precision=exact_precision,
        )
        local_coeffs = group_sum(partial_value) / row_count
        correction = jnp.einsum("kcxyz,kn->ncxyz", basis, local_coeffs, precision=exact_precision)
        fine_block = fine_block - lax.psum_scatter(
            correction, "basis", scatter_dimension=3, tiled=True
        )
        running = running + local_coeffs
    orthonormal, upper_factor = finish(fine_block, row_count)
    return (orthonormal, running, upper_factor)


def solution(mesh):
    in_specs = (
        P(None, None, "space", "basis", None),
        P("basis", None, "space", None, None),
        P("space", "basis", None),
        P(),
        P(),
        P(),
        P(),
        P(),
        P(),
        P(),
    )
    out_specs = (P(None, None, "space", "basis", None), P("basis", None), P())
    return jax.shard_map(shards, mesh=mesh, in_specs=in_specs, out_specs=out_specs, check_vma=False)
```

profile of v0, /device:TPU:1, one launch (start us, length us, event | category | flops | bytes accessed | tf_op | source)
XLA Modules:
  0.0 749.9 jit_solution(10074327521690366731)
XLA Ops:
  7.2 0.0 copy-start
  7.2 0.0 reduce-scatter.9.cloned.1.call-start
  7.3 1.0 copy.71
  8.3 8.8 %collective-permute-start.1 = (f32[16,3,1,8,128]{4,0,3,1,2:T(8,128)S(1)}, f32[16,3,1,8,128]{4,0,3,1,2:T(8,128)S(1)}, u32[]{:S(2)}, u32[]{:S(2)}) collective-permute-start(f32[16,3,1,8,128]{4,0,3,1,2:T(8,128)S(1)} %copy.71), channel_id=1, source_target_pairs={{4,0},{8,4},{12,8},{16,12},{20,16},{24,20},{28,24},{32,28},{36,32}... | collective-permute-start | bytes 589832 | tf_op jit(solution)/shard_map/ppermute | solution.py:19
  17.1 1.9 collective-permute-start
  19.0 0.0 copy-start.3
  19.0 0.0 copy-start.2
  19.7 1.3 dynamic-slice.13
  21.0 1.3 dynamic-slice.12
  23.6 0.0 copy-done.4
  23.6 0.1 slice_add_fusion
  23.7 0.1 scatter-add.4
  23.9 0.1 copy.94
  24.0 0.1 copy.101
  24.1 0.1 copy.100
  24.2 0.1 copy.99
  24.3 0.1 copy.98
  24.4 0.1 copy.97
  24.5 0.1 copy.96
  24.6 0.1 copy.95
  24.7 0.6 multiply_add_fusion
  25.4 0.1 fusion.22
  25.5 0.0 copy-start.1
  25.5 0.0 collective-permute-done
  25.6 0.9 copy-done.1
  26.5 0.0 collective-permute-done.1
  26.6 1.3 collective-permute-start.3
  27.9 4.0 collective-permute-start.2
  31.9 0.0 collective-permute-done.3
  31.9 1.4 collective-permute-done.2
  33.2 0.2 add_add_fusion.2
  33.4 0.2 add_add_fusion.1
  33.7 0.2 add_add_fusion
  33.9 11.9 %all_gather.6 = f32[16,3,1,32,128]{4,0,3,1,2:T(8,128)S(1)} all-gather(f32[16,3,1,8,128]{4,0,3,1,2:T(8,128)S(1)} %pad_maximum_fusion), channel_id=1, replica_groups=mesh['space'=128,'basis'=4] {'basis'}, dimensions={3}, use_global_device_ids=true | all-gather | bytes 983040 | tf_op jit(solution)/shard_map/all_gather | solution.py:109
  45.8 1.4 convolution_bitcast_fusion.4
  47.2 256.7 %psum.21 = f32[16,16]{0,1:T(8,128)S(1)} all-reduce(f32[16,16]{0,1:T(8,128)S(1)} %convolution_bitcast_fusion.4), channel_id=1, replica_groups=mesh['space'=128,'basis'=4] {'space'}, use_global_device_ids=true, to_apply=%region_0.1 | all-reduce | flops 256 | bytes 2048 | tf_op jit(solution)/shard_map/psum | solution.py:74
  303.9 1.1 convolution_bitcast_fusion.1
  305.0 0.1 copy.103
  305.1 1.1 copy.129
  306.2 0.0 reduce-scatter.9.cloned.1.call-update
  306.3 0.0 reduce-scatter.11.cloned.1.call-start
  306.3 26.9 %reduce-scatter.9.cloned.1.call-done = f32[8,6144]{1,0:T(8,128)} async-done(((f32[32,6144]{1,0:T(8,128)}), f32[8,6144]{1,0:T(8,128)}) %reduce-scatter.9.cloned.1.call-update) | async-done | bytes 196624
  333.2 1.0 copy.108
  334.2 11.1 %all_gather.7 = f32[16,3,1,32,128]{4,0,3,1,2:T(8,128)S(1)} all-gather(f32[16,3,1,8,128]{4,0,3,1,2:T(8,128)S(1)} %copy_subtract_fusion.1), channel_id=1, replica_groups=mesh['space'=128,'basis'=4] {'basis'}, dimensions={3}, use_global_device_ids=true | all-gather | bytes 983040 | tf_op jit(solution)/shard_map/all_gather | solution.py:109
  345.3 1.4 convolution_bitcast_fusion.3
  346.7 256.0 %psum.22 = f32[16,16]{0,1:T(8,128)S(1)} all-reduce(f32[16,16]{0,1:T(8,128)S(1)} %convolution_bitcast_fusion.3), channel_id=1, replica_groups=mesh['space'=128,'basis'=4] {'space'}, use_global_device_ids=true, to_apply=%region_2.3 | all-reduce | flops 256 | bytes 2048 | tf_op jit(solution)/shard_map/psum | solution.py:74
  602.7 1.1 convolution_bitcast_fusion
  603.9 0.1 copy.105
  603.9 1.1 copy.128
  605.1 0.0 reduce-scatter.11.cloned.1.call-update
  605.1 0.7 copy.86
  605.8 24.7 %reduce-scatter.11.cloned.1.call-done = f32[8,6144]{1,0:T(8,128)} async-done(((f32[32,6144]{1,0:T(8,128)}), f32[8,6144]{1,0:T(8,128)}) %reduce-scatter.11.cloned.1.call-update) | async-done | bytes 196624
  630.5 1.0 copy.110
  631.5 0.3 convolution_bitcast_fusion.6
  631.8 105.2 %psum.23 = f32[16,16]{0,1:T(8,128)S(1)} all-reduce(f32[16,16]{0,1:T(8,128)S(1)} %convolution_bitcast_fusion.6), channel_id=1, replica_groups=mesh['space'=128,'basis'=4] {'space','basis'}, use_global_device_ids=true, to_apply=%region_4.5 | all-reduce | flops 256 | bytes 2048 | tf_op jit(solution)/shard_map/psum | solution.py:89
  737.0 0.1 copy.84
  737.1 1.5 cholesky.17
  738.6 0.6 compare_reduce_fusion
  739.2 0.6 fusion.15
  739.9 0.7 copy.87
  740.6 1.2 custom-call.7
  741.8 0.2 convolution_bitcast_fusion.5
  742.0 0.3 convolution_bitcast_fusion.2
  742.3 0.7 copy.85
  (27 shorter events, 0.3 us)
Async XLA Ops:
  7.2 38.7 %copy-start = (f32[16,3,1,32,128]{4,3,2,1,0:T(8,128)S(1)}, f32[16,3,1,32,128]{4,3,2,1,0:T(8,128)}, u32[]{:S(2)}) copy-start(f32[16,3,1,32,128]{4,3,2,1,0:T(8,128)} %param.13) | copy-start | bytes 2359300
  7.2 326.0 %reduce-scatter.9.cloned.1.call-start = ((), (), s32[]{:S(2)}) async-start(), calls=%async_computation.2 | async-start | bytes 983040
  7.2 16.3 %copy-start.4 = (s32[1,8,128]{2,1,0:T(8,128)S(1)}, s32[1,8,128]{2,1,0:T(8,128)}, u32[]{:S(2)}) copy-start(s32[1,8,128]{2,1,0:T(8,128)} %param.14) | copy-start | bytes 12292
  7.2 16.3 %copy-start.5 = (f32[8,3]{0,1:T(4,128)S(1)}, f32[8,3]{0,1:T(4,128)}, u32[]{:S(2)}) copy-start(f32[8,3]{0,1:T(4,128)} %param.16) | copy-start | bytes 292
  7.2 16.3 %copy-start.6 = (f32[8,3]{0,1:T(4,128)S(1)}, f32[8,3]{0,1:T(4,128)}, u32[]{:S(2)}) copy-start(f32[8,3]{0,1:T(4,128)} %param.18) | copy-start | bytes 292
  8.3 18.2 %collective-permute-start.1 = (f32[16,3,1,8,128]{4,0,3,1,2:T(8,128)S(1)}, f32[16,3,1,8,128]{4,0,3,1,2:T(8,128)S(1)}, u32[]{:S(2)}, u32[]{:S(2)}) collective-permute-start(f32[16,3,1,8,128]{4,0,3,1,2:T(8,128)S(1)} %copy.71), channel_id=1, source_target_pairs={{4,0},{8,4},{12,8},{16,12},{20,16},{24,20},{28,24},{32,28},{36,32}... | collective-permute-start | bytes 589832 | tf_op jit(solution)/shard_map/ppermute | solution.py:19
  17.1 8.5 %collective-permute-start = (f32[16,3,1,8,128]{4,0,3,1,2:T(8,128)S(1)}, f32[16,3,1,8,128]{4,0,3,1,2:T(8,128)S(1)}, u32[]{:S(2)}, u32[]{:S(2)}) collective-permute-start(f32[16,3,1,8,128]{4,0,3,1,2:T(8,128)S(1)} %copy.71), channel_id=1, source_target_pairs={{0,4},{4,8},{8,12},{12,16},{16,20},{20,24},{24,28},{28,32},{32,36}... | collective-permute-start | bytes 589832 | tf_op jit(solution)/shard_map/ppermute | solution.py:17
  19.0 4.6 copy-start.3
  19.0 4.6 copy-start.2
  25.5 0.9 copy-start.1
  26.6 5.3 collective-permute-start.3
  27.9 5.4 collective-permute-start.2
  306.3 324.3 %reduce-scatter.11.cloned.1.call-start = ((), (), s32[]{:S(2)}) async-start(), calls=%async_computation.3 | async-start | bytes 983040
Sparse Core Ops, SparseCore 0:
  306.4 26.7 reduce-scatter.8
  605.2 25.2 reduce-scatter.10
where the time goes:
time: 750 us
  blocking collectives  641 us (85%)
  waiting for transfers between devices  53 us (7%)
  between operations  16.4 us (2%)
  starting transfers between devices  16.1 us (2%)
  local copies, waits for them, and re-layouts  12.2 us (2%)
    psum x2, blocking collectives, group_sum(): return lax.psum(partial_value, 'space')  513 us
    psum x1, blocking collectives, finish(): gram_matrix = lax.psum(gram_partial, ('space', 'basis')) / row_count  105 us
    unnamed x4, waiting for transfers between devices  51.6 us
    all_gather x2, blocking collectives, shards(): lax.all_gather(fine_block, 'basis', axis=3, tiled=True)  23 us
  transfers between devices with their start and end apart: 6, of which 3 were waited for; matrix products, arithmetic and copies ran while one was open for 1% of the time, Pallas kernels for 0%

commit v1 on v0

v1 whole, which is shorter than its diff:
```python
import functools

import jax
import jax.numpy as jnp
from jax import lax
from jax.experimental import pallas as pl
from jax.experimental.pallas import tpu as pltpu
from jax.sharding import PartitionSpec as P

MESH = pl.DeviceIdType.MESH
PLANE = 8
EXACT = lax.Precision.HIGHEST
F32 = jnp.float32
BF16 = jnp.bfloat16


def dot_exact(a, b):
    return lax.dot_general(
        a, b, (((1,), (0,)), ((), ())), precision=EXACT, preferred_element_type=F32
    )


def iota(shape, axis):
    return lax.broadcasted_iota(jnp.int32, shape, axis)


def pick(bits, values):
    level = list(values)
    for bit in bits:
        level = [jnp.where(bit, level[i + 1], level[i]) for i in range(0, len(level), 2)]
    return level[0]


def fill_fields(mat_ref, k0, ke, diag, mass, velocities, shifts, sample, fields):
    index = sample[0, 0]
    velocity = velocities[index // 128, index % 128]
    shift = shifts[index // 128, index % 128]
    square = velocity * velocity
    cells = mat_ref[0]
    bits = [((cells >> b) & 1) == 1 for b in range(3)]

    def offset_body(o, carry):
        for i in range(3):
            for j in range(3):
                values = [k0[i, j, m, o] - square * ke[i, j, m, o] for m in range(8)]
                fields[o * 9 + i * 3 + j] = pick(bits, values)
        return carry

    lax.fori_loop(0, 7, offset_body, 0)
    for i in range(3):
        values = [diag[i, m] - shift * mass[i, m] for m in range(8)]
        fields[4 * i] = fields[4 * i] + pick(bits, values)


def apply_stencil(xs, xh, yh, fields, applied):
    row = iota((8, 128), 0)
    lane = iota((8, 128), 1)

    def column(n, carry):
        sums = [None] * 3
        for j in range(3):
            centre = xs[n, j]
            low_y = jnp.where(
                row == 0, jnp.broadcast_to(yh[0, n, j], (8, 128)), pltpu.roll(centre, 1, 0)
            )
            high_y = jnp.where(
                row == 7, jnp.broadcast_to(yh[1, n, j], (8, 128)), pltpu.roll(centre, 7, 0)
            )
            low_z = jnp.where(lane == 0, 0.0, pltpu.roll(centre, 1, 1))
            high_z = jnp.where(lane == 127, 0.0, pltpu.roll(centre, 127, 1))
            views = [centre, xh[0, n, j], xh[1, n, j], low_y, high_y, low_z, high_z]
            for o in range(7):
                for i in range(3):
                    term = fields[o * 9 + i * 3 + j] * views[o]
                    sums[i] = term if sums[i] is None else sums[i] + term
        for i in range(3):
            applied[n, i] = sums[i]
        return carry

    lax.fori_loop(0, 16, column, 0)


def split_rows(raw, data, first):
    def tile(t, carry):
        block = raw[pl.ds(t, 16, stride=24), :]
        high = block.astype(BF16)
        rest = (block - high.astype(F32)).astype(BF16)
        lanes = pl.ds(pl.multiple_of(t * 128, 128), 128)
        data[pl.ds(first, 16), lanes] = high
        data[pl.ds(80 + first, 16), lanes] = rest
        return carry

    lax.fori_loop(0, 24, tile, 0, unroll=4)


def pack_upper(full, packed):
    lane = iota((16, 128), 1)
    rows = [full[16 * g : 16 * g + 16, :] for g in range(5)]
    packed[0:16, :] = jnp.where(lane < 80, rows[0], pltpu.roll(rows[2], 48, 1))
    packed[16:32, :] = jnp.where(
        lane < 64,
        pltpu.roll(rows[1], 112, 1),
        jnp.where(
            lane < 96,
            pltpu.roll(rows[3], 16, 1),
            jnp.where(lane < 112, pltpu.roll(rows[4], 32, 1), 0.0),
        ),
    )


def unpack_full(packed, scale):
    lane = iota((16, 128), 1)
    one, two = packed[0:16, :], packed[16:32, :]
    parts = [
        one,
        pltpu.roll(two, 16, 1),
        pltpu.roll(one, 80, 1),
        pltpu.roll(two, 112, 1),
        pltpu.roll(two, 96, 1),
    ]
    rows = []
    for g in range(5):
        weight = jnp.where(lane < 16 * g + 16, 0.5 * scale, scale)
        rows.append(jnp.where((lane >= 16 * g) & (lane < 80), parts[g] * weight, 0.0))
    rows.append(jnp.zeros((48, 128), F32))
    upper = jnp.concatenate(rows, axis=0)
    return upper + upper.T


def factor(gram):
    row = iota((16, 128), 0)
    lane = iota((16, 128), 1)
    work = jnp.where(lane < 16, gram, jnp.where(lane == row + 16, 1.0, 0.0))
    for k in range(15):
        pivot_row = jnp.broadcast_to(work[k : k + 1, :], (16, 128))
        column = jnp.broadcast_to(work[:, k : k + 1], (16, 128))
        pivot = jnp.broadcast_to(work[k : k + 1, k : k + 1], (16, 128))
        work = work - jnp.where(row > k, column / pivot, 0.0) * pivot_row
    pivots = jnp.sum(jnp.where(lane == row, work, 0.0), axis=1, keepdims=True)
    root = lax.rsqrt(pivots)
    root = root * (1.5 - 0.5 * pivots * root * root)
    return work * root


def kernel(
    sizes,
    x_hbm, basis_hbm, mat_hbm, k0_hbm, ke_hbm, diag_hbm, mass_hbm, vel_hbm, shift_hbm, sample_hbm,
    ortho_hbm, coeff_hbm, upper_hbm,
    k0, ke, diag, mass, velocities, shifts, sample,
    mat, xs, xh, yh, raw, applied, fields, data, full, packed, part, zpart, zsum, total, total_z,
    weights, result, coeff, upper,
    local_sems, b_send, b_recv, x_send, x_recv, y_send, y_recv, r_send, r_recv, o_sems,
):
    space, sides, plane, row_count = sizes
    depth = space // plane
    members = sides * plane
    share = 32 // members
    s = lax.axis_index("space")
    b = lax.axis_index("basis")
    z = s // plane
    spot = s - z * plane
    me = b * plane + spot

    def member(k):
        index = lax.rem(me + k, members)
        side = index // plane
        return index, (z * plane + (index - side * plane), side)

    def level(k):
        index = lax.rem(z + k, depth)
        return index, (index * plane + spot, b)

    small = [
        (sample_hbm, sample), (vel_hbm, velocities), (shift_hbm, shifts), (k0_hbm, k0),
        (ke_hbm, ke), (diag_hbm, diag), (mass_hbm, mass), (mat_hbm, mat),
        (x_hbm.at[:, :, 0], xs),
        (basis_hbm.at[:, :, 0, pl.ds(pl.multiple_of(b * 8, 8), 8), :], raw.at[b]),
    ]
    small = [
        pltpu.make_async_copy(source, target, local_sems.at[i])
        for i, (source, target) in enumerate(small)
    ]
    for copy in small:
        copy.start()

    barrier = pltpu.get_barrier_semaphore()

    def greet(peer):
        pl.semaphore_signal(barrier, inc=1, device_id=peer, device_id_type=MESH)

    @pl.loop(1, members)
    def _(k):
        greet(member(k)[1])

    @pl.loop(1, depth)
    def _(k):
        greet(level(k)[1])

    over = (spot == plane - 1) & (z < depth - 1)
    under = (spot == 0) & (z > 0)

    @pl.when(over)
    def _():
        greet((s + 1, b))

    @pl.when(under)
    def _():
        greet((s - 1, b))

    extra = jnp.where(over | under, 1, 0)
    pl.semaphore_wait(barrier, members + depth - 2 + extra)

    def remote(source, target, send, recv, peer):
        return pltpu.make_async_remote_copy(
            src_ref=source, dst_ref=target, send_sem=send, recv_sem=recv,
            device_id=peer, device_id_type=MESH,
        )

    def basis_copy(k):
        side = lax.rem(b + k, sides)
        return remote(
            basis_hbm.at[:, :, 0, pl.ds(pl.multiple_of(side * 8, 8), 8), :],
            raw.at[b], b_send.at[k - 1], b_recv.at[k - 1], (s, side),
        )

    def x_copy(way):
        peer = s + 1 if way == 0 else s - 1
        return remote(x_hbm.at[:, :, 0], xh.at[way], x_send.at[way], x_recv.at[way], (peer, b))

    def y_copy(way):
        peer = b + 1 if way == 0 else b - 1
        edge = 7 if way == 0 else 0
        return remote(
            x_hbm.at[:, :, 0, edge : edge + 1, :], yh.at[way], y_send.at[way], y_recv.at[way],
            (s, peer),
        )

    x_sends = [s < space - 1, s > 0]
    x_gets = [s > 0, s < space - 1]
    y_sends = [b < sides - 1, b > 0]
    y_gets = [b > 0, b < sides - 1]
    for way in range(2):
        pl.when(y_sends[way])(lambda way=way: y_copy(way).start())
    for k in (2, 1, 3):
        basis_copy(k).start()
    for way in range(2):
        pl.when(x_sends[way])(lambda way=way: x_copy(way).start())

    for copy in small[:8]:
        copy.wait()
    fill_fields(mat, k0, ke, diag, mass, velocities, shifts, sample, fields)
    small[9].wait()
    own = pl.multiple_of(b * 16, 16)
    split_rows(raw.at[b].reshape(384, 128), data, own)
    small[8].wait()

    for way in range(2):
        @pl.when(jnp.logical_not(x_gets[way]))
        def _():
            xh[way] = jnp.zeros(xs.shape, F32)

        @pl.when(jnp.logical_not(y_gets[way]))
        def _():
            yh[way] = jnp.zeros((16, 3, 1, 128), F32)

        pl.when(x_gets[way])(lambda way=way: x_copy(way).wait_recv())
        pl.when(y_gets[way])(lambda way=way: y_copy(way).wait_recv())

    apply_stencil(xs, xh, yh, fields, applied)
    split_rows(applied.reshape(384, 128), data, 64)

    for k in (1, 3, 2):
        basis_copy(k).wait_recv()
        side = lax.rem(b + sides - k, sides)
        split_rows(raw.at[side].reshape(384, 128), data, pl.multiple_of(side * 16, 16))

    products = lax.dot_general(
        data[...], data[...], (((1,), (1,)), ((), ())), preferred_element_type=F32
    )
    products = products[0:80] + products[80:160]
    full[:, 0:80] = products[:, 0:80] + products[:, 80:160]
    pack_upper(full, packed)

    def rows_of(index):
        return pl.ds(index * share, share)

    def scatter_copy(k):
        index, peer = member(k)
        return remote(
            packed.at[rows_of(index)], part.at[rows_of(me)], r_send.at[0], r_recv.at[0], peer
        )

    def level_copy(k):
        _, peer = level(k)
        return remote(zpart, zsum.at[rows_of(z)], r_send.at[1], r_recv.at[1], peer)

    def gather_copy(k):
        _, peer = member(k)
        return remote(total_z, total.at[rows_of(me)], r_send.at[2], r_recv.at[2], peer)

    def fold(ref, count):
        if share == 1:
            return jnp.sum(ref[...], axis=0, keepdims=True)
        return functools.reduce(
            lambda a, c: a + c, [ref[m * share : (m + 1) * share] for m in range(count)]
        )

    def wait_rows(ref, count, sem):
        view = ref.at[pl.ds(0, count * share)]
        pltpu.make_async_copy(view, view, sem).wait()

    @pl.loop(1, members)
    def _(k):
        scatter_copy(k).start()

    part[rows_of(me)] = packed[rows_of(me)]
    wait_rows(part, members - 1, r_recv.at[0])
    zpart[...] = fold(part, members)

    @pl.loop(1, depth)
    def _(k):
        level_copy(k).start()

    zsum[rows_of(z)] = zpart[...]
    wait_rows(zsum, depth - 1, r_recv.at[1])
    total_z[...] = fold(zsum, depth)

    @pl.loop(1, members)
    def _(k):
        gather_copy(k).start()

    total[rows_of(me)] = total_z[...]
    wait_rows(total, members - 1, r_recv.at[2])

    moments = unpack_full(total, 1.0 / row_count)
    lane64 = iota((64, 128), 1)
    first = jnp.where(lane64 < 16, pltpu.roll(moments[0:64], 64, 1), 0.0)
    gram_basis = jnp.where(lane64 < 64, moments[0:64], 0.0)
    zeros64 = jnp.zeros((64, 128), F32)
    both = 2.0 * first - dot_exact(gram_basis, jnp.concatenate([first, zeros64], axis=0))
    full[0:64, :] = both
    coeff[...] = full[pl.ds(own, 16), 0:16]
    coeff_out = pltpu.make_async_copy(coeff, coeff_hbm, o_sems.at[0])
    coeff_out.start()
    unit = jnp.where((iota((64, 128), 0) == lane64) & (lane64 < 16), 1.0, 0.0)
    mix = jnp.concatenate([-both, unit], axis=0)
    image = dot_exact(moments, mix)
    mix_t = mix.T[0:16]
    gram = dot_exact(mix_t, image)
    factors = factor(gram)
    upper[...] = jnp.where(iota((16, 16), 0) <= iota((16, 16), 1), factors[:, 0:16], 0.0)
    upper_out = pltpu.make_async_copy(upper, upper_hbm, o_sems.at[1])
    upper_out.start()
    inverse = pltpu.roll(factors, 112, 1)
    inverse = jnp.where(iota((16, 128), 1) < 16, inverse, 0.0)
    weight = dot_exact(
        inverse, jnp.concatenate([mix_t, jnp.zeros((112, 128), F32)], axis=0)
    )
    high = weight.astype(BF16).astype(F32)
    stacked = jnp.concatenate([high, weight - high], axis=0)
    weights[:, 0:80] = stacked[:, 0:80]
    weights[:, 80:160] = stacked[:, 0:80]
    left = weights[:, 0:160].astype(BF16)
    out = result.reshape(384, 128)
    for t in range(0, 24, 2):
        piece = jnp.dot(left, data[:, t * 128 : t * 128 + 256], preferred_element_type=F32)
        piece = piece[0:16] + piece[16:32]
        out[pl.ds(t, 16, stride=24), :] = piece[:, 0:128]
        out[pl.ds(t + 1, 16, stride=24), :] = piece[:, 128:256]
    ortho_out = pltpu.make_async_copy(result, ortho_hbm.at[:, :, 0], o_sems.at[2])
    ortho_out.start()

    for k in (1, 2, 3):
        basis_copy(k).wait_send()
    for way in range(2):
        pl.when(x_sends[way])(lambda way=way: x_copy(way).wait_send())
        pl.when(y_sends[way])(lambda way=way: y_copy(way).wait_send())
    wait_rows(part, members - 1, r_send.at[0])
    wait_rows(zsum, depth - 1, r_send.at[1])
    wait_rows(total, members - 1, r_send.at[2])
    coeff_out.wait()
    upper_out.wait()
    ortho_out.wait()


def shards(space, sides, x_block, basis, material, k0, diag, ke, mass, velocities, shifts, sample):
    plane = PLANE
    share = 32 // (sides * plane)
    depth = space // plane
    row_count = 3.0 * space * x_block.shape[3] * sides * x_block.shape[4]
    vmem, smem, dma = pltpu.VMEM, pltpu.SMEM, pltpu.SemaphoreType.DMA
    block = (16, 3, 8, 128)
    scratch = [
        smem((3, 3, 8, 7), F32), smem((3, 3, 8, 7), F32), smem((3, 8), F32), smem((3, 8), F32),
        smem((8, 128), F32), smem((8, 128), F32), smem((1, 1), jnp.int32),
        vmem((1, 8, 128), jnp.int32), vmem(block, F32), vmem((2,) + block, F32),
        vmem((2, 16, 3, 1, 128), F32), vmem((sides,) + block, F32), vmem(block, F32),
        vmem((63, 8, 128), F32), vmem((160, 3072), BF16), vmem((80, 128), F32),
        vmem((32, 128), F32), vmem((32, 128), F32), vmem((share, 128), F32),
        vmem((depth * share, 128), F32), vmem((32, 128), F32), vmem((share, 128), F32),
        vmem((32, 256), F32), vmem(block, F32), vmem((16, 16), F32), vmem((16, 16), F32),
        dma((10,)), dma((3,)), dma((3,)), dma((2,)), dma((2,)), dma((2,)), dma((2,)),
        dma((3,)), dma((3,)), dma((3,)),
    ]
    whole = pl.BlockSpec(memory_space=pltpu.HBM)
    return pl.pallas_call(
        functools.partial(kernel, (space, sides, plane, row_count)),
        out_shape=(
            jax.ShapeDtypeStruct(x_block.shape, F32),
            jax.ShapeDtypeStruct((16, 16), F32),
            jax.ShapeDtypeStruct((16, 16), F32),
        ),
        in_specs=[whole] * 10,
        out_specs=(whole,) * 3,
        scratch_shapes=scratch,
        compiler_params=pltpu.CompilerParams(
            collective_id=0, has_side_effects=True, vmem_limit_bytes=64 * 1024 * 1024
        ),
    )(
        x_block, basis, material,
        jnp.transpose(k0, (2, 3, 0, 1)), jnp.transpose(ke, (2, 3, 0, 1)),
        diag.T, mass.T, velocities.reshape(8, 128), shifts.reshape(8, 128), sample.reshape(1, 1),
    )


def solution(mesh):
    in_specs = (
        P(None, None, "space", "basis", None), P("basis", None, "space", None, None),
        P("space", "basis", None), P(), P(), P(), P(), P(), P(), P(),
    )
    out_specs = (P(None, None, "space", "basis", None), P("basis", None), P())
    body = functools.partial(shards, mesh.shape["space"], mesh.shape["basis"])
    return jax.shard_map(body, mesh=mesh, in_specs=in_specs, out_specs=out_specs, check_vma=False)
```

time: 750 us -> 53.4 us (0.07)
  blocking collectives: 641 us -> 0 us
  waiting for transfers between devices: 53 us -> 0 us
  Pallas kernels: 0 us -> 49 us
  starting transfers between devices: 16.1 us -> 0 us
  between operations: 16.4 us -> 1.3 us
  local copies, waits for them, and re-layouts: 12.2 us -> 2.93 us
    psum x3 -> x0, blocking collectives: 618 us -> none  [the longest x2 513 us: group_sum(): return lax.psum(partial_value, 'space')]
    unnamed x4 -> x0, waiting for transfers between devices: 51.6 us -> none
    pallas_call x0 -> x1, Pallas kernels: none -> 49 us  [shards(): pl.pallas_call(functools.partial(kernel, (space, sides, plane, row_count)...]
    all_gather x2 -> x0, blocking collectives: 23 us -> none  [shards(): lax.all_gather(fine_block, 'basis', axis=3, tiled=True)]
    ppermute x4 -> x0, starting transfers between devices: 16 us -> none  [the longest x2 10.1 us: with_halo(): lax.ppermute(head, axis, [((i + 1) % count, i) for i in range(ends)])]
  transfers between devices with their start and end apart: 6 -> 0, of which waited for: 3 -> 0; matrix products, arithmetic and copies ran while one was open for 1% -> 0% of each run, Pallas kernels for 0% -> 0%
where the time goes in v1:
time: 53.4 us; the launch traced here: 53.2 us
  Pallas kernels  49 us (92%)
  local copies, waits for them, and re-layouts  2.93 us (5%)
  between operations  1.3 us (2%)
    pallas_call x1, Pallas kernels, shards(): pl.pallas_call(functools.partial(kernel, (space, sides, plane, row_count)...  49 us
    unnamed x7, local copies, waits for them, and re-layouts  2.93 us

profile of v1, /device:TPU:1, one launch (start us, length us, event | category | flops | bytes accessed | tf_op | source)
XLA Modules:
  0.0 53.2 jit_solution(15702545084487263821)
XLA Ops:
  1.3 49.0 %shard_map.121 = (f32[16,3,1,8,128]{4,3,2,1,0:T(8,128)}, f32[16,16]{1,0:T(8,128)}, f32[16,16]{1,0:T(8,128)}) custom-call(f32[16,3,1,8,128]{4,3,2,1,0:T(8,128)} %x_hbm.1, f32[16,3,1,32,128]{4,3,2,1,0:T(8,128)} %basis_hbm.1, s32[1,8,128]{2,1,0:T(8,128)} %mat_hbm.1, f32[3,3,8,7]{3,2,1,0:T(8,128)} %bitcast.8, f32[3,3,8,7]{3,2,1,0:T(8,128)} %bitcast.9, ...), custom_call_target="tpu_custom_call" | custom-call | tf_op jit(solution)/shard_map/pallas_call | solution.py:406
  50.3 0.0 copy-start.1
  50.3 1.6 %copy.17 = f32[16,3,1,8,128]{4,3,2,1,0:T(8,128)} copy(f32[16,3,1,8,128]{4,3,2,1,0:T(8,128)} %get-tuple-element.6) | data formatting | bytes 393216
  51.9 0.0 copy-done.1
  51.9 0.0 copy-start
  51.9 0.6 %copy.18 = f32[16,16]{1,0:T(8,128)} copy(f32[16,16]{1,0:T(8,128)S(1)} %copy-done.1) | data formatting | bytes 2048
  52.5 0.1 copy-done
  52.6 0.6 %copy.19 = f32[16,16]{1,0:T(8,128)} copy(f32[16,16]{1,0:T(8,128)S(1)} %copy-done) | data formatting | bytes 2048
Async XLA Ops:
  50.3 1.6 %copy-start.1 = (f32[16,16]{1,0:T(8,128)S(1)}, f32[16,16]{1,0:T(8,128)}, u32[]{:S(2)}) copy-start(f32[16,16]{1,0:T(8,128)} %get-tuple-element.7) | copy-start | bytes 3076
  51.9 0.7 %copy-start = (f32[16,16]{1,0:T(8,128)S(1)}, f32[16,16]{1,0:T(8,128)}, u32[]{:S(2)}) copy-start(f32[16,16]{1,0:T(8,128)} %get-tuple-element.8) | copy-start | bytes 3076

commit v2 on v1

--- a/solution.py
+++ b/solution.py
@@ -32,7 +32,7 @@
 
 
 def fill_fields(mat_ref, k0, ke, diag, mass, velocities, shifts, sample, fields):
-    index = sample[0, 0]
+    index = sample[0]
     velocity = velocities[index // 128, index % 128]
     shift = shifts[index // 128, index % 128]
     square = velocity * velocity
@@ -80,8 +80,9 @@
     lax.fori_loop(0, 16, column, 0)
 
 
-def split_rows(raw, data, first):
-    def tile(t, carry):
+def split_rows(raw, data, first, part):
+    def tile(i, carry):
+        t = part * 8 + i
         block = raw[pl.ds(t, 16, stride=24), :]
         high = block.astype(BF16)
         rest = (block - high.astype(F32)).astype(BF16)
@@ -90,7 +91,7 @@
         data[pl.ds(80 + first, 16), lanes] = rest
         return carry
 
-    lax.fori_loop(0, 24, tile, 0, unroll=4)
+    lax.fori_loop(0, 8, tile, 0, unroll=True)
 
 
 def pack_upper(full, packed):
@@ -144,34 +145,58 @@
 
 def kernel(
     sizes,
-    x_hbm, basis_hbm, mat_hbm, k0_hbm, ke_hbm, diag_hbm, mass_hbm, vel_hbm, shift_hbm, sample_hbm,
-    ortho_hbm, coeff_hbm, upper_hbm,
-    k0, ke, diag, mass, velocities, shifts, sample,
-    mat, xs, xh, yh, raw, applied, fields, data, full, packed, part, zpart, zsum, total, total_z,
-    weights, result, coeff, upper,
+    x_hbm, basis_hbm, mat_hbm, k0_hbm, ke_hbm, diag_hbm, mass_hbm, vel_hbm, shift_hbm, sample,
+    total, data_hbm,
+    k0, ke, diag, mass, velocities, shifts,
+    mat, xs, xh, yh, raw, applied, fields, data, full, packed, part, zpart, zsum, total_z,
     local_sems, b_send, b_recv, x_send, x_recv, y_send, y_recv, r_send, r_recv, o_sems,
 ):
     space, sides, plane, row_count = sizes
     depth = space // plane
     members = sides * plane
     share = 32 // members
+    lines = plane // 2
     s = lax.axis_index("space")
     b = lax.axis_index("basis")
     z = s // plane
     spot = s - z * plane
+    x = spot // 2
+    core = spot - 2 * x
     me = b * plane + spot
 
-    def member(k):
-        index = lax.rem(me + k, members)
-        side = index // plane
-        return index, (z * plane + (index - side * plane), side)
-
-    def level(k):
-        index = lax.rem(z + k, depth)
-        return index, (index * plane + spot, b)
+    def members_each(act):
+        sites = [(dx, dy) for dx in range(lines) for dy in range(sides)]
+        sites.sort(key=lambda d: -(min(d[0], lines - d[0]) + min(d[1], sides - d[1])))
+        for dx, dy in sites:
+            column, side = lax.rem(x + dx, lines), lax.rem(b + dy, sides)
+            for other in ((1 - core, core) if dx or dy else (1 - core,)):
+                index = side * plane + column * 2 + other
+                act(index, (z * plane + column * 2 + other, side))
+
+    def levels_each(act):
+        far = depth // 2
+        act((lax.rem(z + far, depth) * plane + spot, b))
+        for d in range(far - 1, 0, -1):
+            act((lax.rem(z + d, depth) * plane + spot, b))
+            act((lax.rem(z + depth - d, depth) * plane + spot, b))
+
+    barrier = pltpu.get_barrier_semaphore()
+
+    def greet(peer):
+        pl.semaphore_signal(barrier, inc=1, device_id=peer, device_id_type=MESH)
+
+    over = (spot == plane - 1) & (z < depth - 1)
+    under = (spot == 0) & (z > 0)
+    levels_each(greet)
+
+    @pl.when(over | under)
+    def _():
+        greet((jnp.where(over, s + 1, s - 1), b))
+
+    members_each(lambda index, peer: greet(peer))
 
     small = [
-        (sample_hbm, sample), (vel_hbm, velocities), (shift_hbm, shifts), (k0_hbm, k0),
+        (vel_hbm, velocities), (shift_hbm, shifts), (k0_hbm, k0),
         (ke_hbm, ke), (diag_hbm, diag), (mass_hbm, mass), (mat_hbm, mat),
         (x_hbm.at[:, :, 0], xs),
         (basis_hbm.at[:, :, 0, pl.ds(pl.multiple_of(b * 8, 8), 8), :], raw.at[b]),
@@ -183,30 +208,6 @@
     for copy in small:
         copy.start()
 
-    barrier = pltpu.get_barrier_semaphore()
-
-    def greet(peer):
-        pl.semaphore_signal(barrier, inc=1, device_id=peer, device_id_type=MESH)
-
-    @pl.loop(1, members)
-    def _(k):
-        greet(member(k)[1])
-
-    @pl.loop(1, depth)
-    def _(k):
-        greet(level(k)[1])
-
-    over = (spot == plane - 1) & (z < depth - 1)
-    under = (spot == 0) & (z > 0)
-
-    @pl.when(over)
-    def _():
-        greet((s + 1, b))
-
-    @pl.when(under)
-    def _():
-        greet((s - 1, b))
-
     extra = jnp.where(over | under, 1, 0)
     pl.semaphore_wait(barrier, members + depth - 2 + extra)
 
@@ -216,11 +217,11 @@
             device_id=peer, device_id_type=MESH,
         )
 
-    def basis_copy(k):
+    def basis_copy(k, c):
         side = lax.rem(b + k, sides)
         return remote(
-            basis_hbm.at[:, :, 0, pl.ds(pl.multiple_of(side * 8, 8), 8), :],
-            raw.at[b], b_send.at[k - 1], b_recv.at[k - 1], (s, side),
+            basis_hbm.at[:, c, 0, pl.ds(pl.multiple_of(side * 8, 8), 8), :],
+            raw.at[b, :, c], b_send.at[k - 1, c], b_recv.at[k - 1, c], (s, side),
         )
 
     def x_copy(way):
@@ -241,18 +242,20 @@
     y_gets = [b > 0, b < sides - 1]
     for way in range(2):
         pl.when(y_sends[way])(lambda way=way: y_copy(way).start())
-    for k in (2, 1, 3):
-        basis_copy(k).start()
+    for c in range(3):
+        for k in (2, 1, 3):
+            basis_copy(k, c).start()
     for way in range(2):
         pl.when(x_sends[way])(lambda way=way: x_copy(way).start())
 
-    for copy in small[:8]:
+    for copy in small[:7]:
         copy.wait()
     fill_fields(mat, k0, ke, diag, mass, velocities, shifts, sample, fields)
-    small[9].wait()
+    small[8].wait()
     own = pl.multiple_of(b * 16, 16)
-    split_rows(raw.at[b].reshape(384, 128), data, own)
-    small[8].wait()
+    for c in range(3):
+        split_rows(raw.at[b].reshape(384, 128), data, own, c)
+    small[7].wait()
 
     for way in range(2):
         @pl.when(jnp.logical_not(x_gets[way]))
@@ -267,36 +270,40 @@
         pl.when(y_gets[way])(lambda way=way: y_copy(way).wait_recv())
 
     apply_stencil(xs, xh, yh, fields, applied)
-    split_rows(applied.reshape(384, 128), data, 64)
-
-    for k in (1, 3, 2):
-        basis_copy(k).wait_recv()
-        side = lax.rem(b + sides - k, sides)
-        split_rows(raw.at[side].reshape(384, 128), data, pl.multiple_of(side * 16, 16))
-
-    products = lax.dot_general(
-        data[...], data[...], (((1,), (1,)), ((), ())), preferred_element_type=F32
-    )
+    for c in range(3):
+        split_rows(applied.reshape(384, 128), data, 64, c)
+
+    products = None
+    for c in range(3):
+        for k in (1, 3, 2):
+            basis_copy(k, c).wait_recv()
+            side = lax.rem(b + sides - k, sides)
+            split_rows(raw.at[side].reshape(384, 128), data, pl.multiple_of(side * 16, 16), c)
+        piece = data[:, c * 1024 : (c + 1) * 1024]
+        term = lax.dot_general(
+            piece, piece, (((1,), (1,)), ((), ())), preferred_element_type=F32
+        )
+        products = term if products is None else products + term
     products = products[0:80] + products[80:160]
     full[:, 0:80] = products[:, 0:80] + products[:, 80:160]
     pack_upper(full, packed)
 
+    data_out = pltpu.make_async_copy(data, data_hbm, o_sems.at[0])
+    data_out.start()
+
     def rows_of(index):
         return pl.ds(index * share, share)
 
-    def scatter_copy(k):
-        index, peer = member(k)
-        return remote(
+    def scatter(index, peer):
+        remote(
             packed.at[rows_of(index)], part.at[rows_of(me)], r_send.at[0], r_recv.at[0], peer
-        )
-
-    def level_copy(k):
-        _, peer = level(k)
-        return remote(zpart, zsum.at[rows_of(z)], r_send.at[1], r_recv.at[1], peer)
-
-    def gather_copy(k):
-        _, peer = member(k)
-        return remote(total_z, total.at[rows_of(me)], r_send.at[2], r_recv.at[2], peer)
+        ).start()
+
+    def along(peer):
+        remote(zpart, zsum.at[rows_of(z)], r_send.at[1], r_recv.at[1], peer).start()
+
+    def gather(index, peer):
+        remote(total_z, total.at[rows_of(me)], r_send.at[2], r_recv.at[2], peer).start()
 
     def fold(ref, count):
         if share == 1:
@@ -309,29 +316,43 @@
         view = ref.at[pl.ds(0, count * share)]
         pltpu.make_async_copy(view, view, sem).wait()
 
-    @pl.loop(1, members)
-    def _(k):
-        scatter_copy(k).start()
-
+    members_each(scatter)
     part[rows_of(me)] = packed[rows_of(me)]
     wait_rows(part, members - 1, r_recv.at[0])
     zpart[...] = fold(part, members)
-
-    @pl.loop(1, depth)
-    def _(k):
-        level_copy(k).start()
-
+    levels_each(along)
     zsum[rows_of(z)] = zpart[...]
     wait_rows(zsum, depth - 1, r_recv.at[1])
     total_z[...] = fold(zsum, depth)
-
-    @pl.loop(1, members)
-    def _(k):
-        gather_copy(k).start()
-
-    total[rows_of(me)] = total_z[...]
+    members_each(gather)
+    own_rows = pltpu.make_async_copy(total_z, total.at[rows_of(me)], o_sems.at[1])
+    own_rows.start()
     wait_rows(total, members - 1, r_recv.at[2])
-
+    own_rows.wait()
+    data_out.wait()
+    for c in range(3):
+        for k in (1, 2, 3):
+            basis_copy(k, c).wait_send()
+    for way in range(2):
+        pl.when(x_sends[way])(lambda way=way: x_copy(way).wait_send())
+        pl.when(y_sends[way])(lambda way=way: y_copy(way).wait_send())
+    wait_rows(part, members - 1, r_send.at[0])
+    wait_rows(zsum, depth - 1, r_send.at[1])
+    wait_rows(total, members - 1, r_send.at[2])
+
+
+def finish(
+    row_count,
+    total_hbm, data_hbm, ortho_hbm, coeff_hbm, upper_hbm,
+    total, data, full, weights, result, coeff, upper, i_sems, o_sems,
+):
+    total_in = pltpu.make_async_copy(total_hbm, total, i_sems.at[0])
+    total_in.start()
+    data_in = pltpu.make_async_copy(data_hbm, data, i_sems.at[1])
+    data_in.start()
+    own = pl.multiple_of(lax.axis_index("basis") * 16, 16)
+
+    total_in.wait()
     moments = unpack_full(total, 1.0 / row_count)
     lane64 = iota((64, 128), 1)
     first = jnp.where(lane64 < 16, pltpu.roll(moments[0:64], 64, 1), 0.0)
@@ -360,6 +381,7 @@
     stacked = jnp.concatenate([high, weight - high], axis=0)
     weights[:, 0:80] = stacked[:, 0:80]
     weights[:, 80:160] = stacked[:, 0:80]
+    data_in.wait()
     left = weights[:, 0:160].astype(BF16)
     out = result.reshape(384, 128)
     for t in range(0, 24, 2):
@@ -369,15 +391,6 @@
         out[pl.ds(t + 1, 16, stride=24), :] = piece[:, 128:256]
     ortho_out = pltpu.make_async_copy(result, ortho_hbm.at[:, :, 0], o_sems.at[2])
     ortho_out.start()
-
-    for k in (1, 2, 3):
-        basis_copy(k).wait_send()
-    for way in range(2):
-        pl.when(x_sends[way])(lambda way=way: x_copy(way).wait_send())
-        pl.when(y_sends[way])(lambda way=way: y_copy(way).wait_send())
-    wait_rows(part, members - 1, r_send.at[0])
-    wait_rows(zsum, depth - 1, r_send.at[1])
-    wait_rows(total, members - 1, r_send.at[2])
     coeff_out.wait()
     upper_out.wait()
     ortho_out.wait()
@@ -392,26 +405,24 @@
     block = (16, 3, 8, 128)
     scratch = [
         smem((3, 3, 8, 7), F32), smem((3, 3, 8, 7), F32), smem((3, 8), F32), smem((3, 8), F32),
-        smem((8, 128), F32), smem((8, 128), F32), smem((1, 1), jnp.int32),
+        smem((8, 128), F32), smem((8, 128), F32),
         vmem((1, 8, 128), jnp.int32), vmem(block, F32), vmem((2,) + block, F32),
         vmem((2, 16, 3, 1, 128), F32), vmem((sides,) + block, F32), vmem(block, F32),
         vmem((63, 8, 128), F32), vmem((160, 3072), BF16), vmem((80, 128), F32),
         vmem((32, 128), F32), vmem((32, 128), F32), vmem((share, 128), F32),
-        vmem((depth * share, 128), F32), vmem((32, 128), F32), vmem((share, 128), F32),
-        vmem((32, 256), F32), vmem(block, F32), vmem((16, 16), F32), vmem((16, 16), F32),
-        dma((10,)), dma((3,)), dma((3,)), dma((2,)), dma((2,)), dma((2,)), dma((2,)),
-        dma((3,)), dma((3,)), dma((3,)),
+        vmem((depth * share, 128), F32), vmem((share, 128), F32),
+        dma((9,)), dma((3, 3)), dma((3, 3)), dma((2,)), dma((2,)), dma((2,)), dma((2,)),
+        dma((3,)), dma((3,)), dma((2,)),
     ]
     whole = pl.BlockSpec(memory_space=pltpu.HBM)
-    return pl.pallas_call(
+    outs = pl.pallas_call(
         functools.partial(kernel, (space, sides, plane, row_count)),
         out_shape=(
-            jax.ShapeDtypeStruct(x_block.shape, F32),
-            jax.ShapeDtypeStruct((16, 16), F32),
-            jax.ShapeDtypeStruct((16, 16), F32),
+            jax.ShapeDtypeStruct((32, 128), F32),
+            jax.ShapeDtypeStruct((160, 3072), BF16),
         ),
-        in_specs=[whole] * 10,
-        out_specs=(whole,) * 3,
+        in_specs=[whole] * 9 + [pl.BlockSpec(memory_space=smem)],
+        out_specs=(whole,) * 2,
         scratch_shapes=scratch,
         compiler_params=pltpu.CompilerParams(
             collective_id=0, has_side_effects=True, vmem_limit_bytes=64 * 1024 * 1024
@@ -419,8 +430,24 @@
     )(
         x_block, basis, material,
         jnp.transpose(k0, (2, 3, 0, 1)), jnp.transpose(ke, (2, 3, 0, 1)),
-        diag.T, mass.T, velocities.reshape(8, 128), shifts.reshape(8, 128), sample.reshape(1, 1),
+        diag.T, mass.T, velocities.reshape(8, 128), shifts.reshape(8, 128), sample,
     )
+    return pl.pallas_call(
+        functools.partial(finish, row_count),
+        out_shape=(
+            jax.ShapeDtypeStruct(x_block.shape, F32),
+            jax.ShapeDtypeStruct((16, 16), F32),
+            jax.ShapeDtypeStruct((16, 16), F32),
+        ),
+        in_specs=[whole] * 2,
+        out_specs=(whole,) * 3,
+        scratch_shapes=[
+            vmem((32, 128), F32), vmem((160, 3072), BF16), vmem((80, 128), F32),
+            vmem((32, 256), F32), vmem(block, F32), vmem((16, 16), F32), vmem((16, 16), F32),
+            dma((2,)), dma((3,)),
+        ],
+        compiler_params=pltpu.CompilerParams(vmem_limit_bytes=64 * 1024 * 1024),
+    )(*outs)
 
 
 def solution(mesh):

time: 53.4 us -> 50.1 us (0.938)
  local copies, waits for them, and re-layouts: 2.93 us -> 0 us
    pallas_call x1, Pallas kernels: 49 us -> 44.1 us  [shards(): pl.pallas_call(functools.partial(kernel, (space, sides, plane, row_count)...]
    pallas_call x0 -> x1, Pallas kernels: none -> 4.56 us  [shards(): pl.pallas_call(functools.partial(finish, row_count), out_shape=(jax.Shape...]
    unnamed x7 -> x0, local copies, waits for them, and re-layouts: 2.93 us -> none
where the time goes in v2:
time: 50.1 us; the launch traced here: 49.9 us
  Pallas kernels  48.6 us (97%)
  between operations  1.29 us (3%)
    pallas_call x1, Pallas kernels, shards(): pl.pallas_call(functools.partial(kernel, (space, sides, plane, row_count)...  44.1 us
    pallas_call x1, Pallas kernels, shards(): pl.pallas_call(functools.partial(finish, row_count), out_shape=(jax.Shape...  4.56 us

profile of v2, /device:TPU:1, one launch (start us, length us, event | category | flops | bytes accessed | tf_op | source)
XLA Modules:
  0.0 49.9 jit_solution(18323889140022929506)
XLA Ops:
  1.3 44.1 %shard_map.121 = (f32[32,128]{1,0:T(8,128)}, bf16[160,3072]{1,0:T(8,128)(2,1)}) custom-call(f32[16,3,1,8,128]{4,3,2,1,0:T(8,128)} %x_hbm.1, f32[16,3,1,32,128]{4,3,2,1,0:T(8,128)} %basis_hbm.1, s32[1,8,128]{2,1,0:T(8,128)} %mat_hbm.1, f32[3,3,8,7]{3,2,1,0:T(8,128)} %bitcast.6, f32[3,3,8,7]{3,2,1,0:T(8,128)} %bitcast.7, f32[3,8]{1,0:T(4,128)} %bitcast.10, ...), custom_call_target="tpu_custom_call" | custom-call | tf_op jit(solution)/shard_map/pallas_call | solution.py:418
  45.4 4.6 %shard_map.122 = (f32[16,3,1,8,128]{4,3,2,1,0:T(8,128)}, f32[16,16]{1,0:T(8,128)}, f32[16,16]{1,0:T(8,128)}) custom-call(f32[32,128]{1,0:T(8,128)} %get-tuple-element.5.total_hbm, bf16[160,3072]{1,0:T(8,128)(2,1)} %get-tuple-element.6.data_hbm), custom_call_target="tpu_custom_call" | custom-call | tf_op jit(solution)/shard_map/pallas_call | solution.py:435

commit v3 on v2

--- a/solution.py
+++ b/solution.py
@@ -9,6 +9,7 @@
 
 MESH = pl.DeviceIdType.MESH
 PLANE = 8
+HOLDERS = 2
 EXACT = lax.Precision.HIGHEST
 F32 = jnp.float32
 BF16 = jnp.bfloat16
@@ -128,19 +129,32 @@
     return upper + upper.T
 
 
-def factor(gram):
-    row = iota((16, 128), 0)
-    lane = iota((16, 128), 1)
-    work = jnp.where(lane < 16, gram, jnp.where(lane == row + 16, 1.0, 0.0))
-    for k in range(15):
-        pivot_row = jnp.broadcast_to(work[k : k + 1, :], (16, 128))
-        column = jnp.broadcast_to(work[:, k : k + 1], (16, 128))
-        pivot = jnp.broadcast_to(work[k : k + 1, k : k + 1], (16, 128))
-        work = work - jnp.where(row > k, column / pivot, 0.0) * pivot_row
-    pivots = jnp.sum(jnp.where(lane == row, work, 0.0), axis=1, keepdims=True)
-    root = lax.rsqrt(pivots)
-    root = root * (1.5 - 0.5 * pivots * root * root)
-    return work * root
+def factor(gram, spread, lines):
+    lane = iota((8, 128), 1)
+    for j in range(16):
+        spread[16 * j : 16 * j + 16, :] = jnp.broadcast_to(gram[:, j : j + 1], (16, 128))
+    lines[...] = gram
+
+    def full(ref, r):
+        return jnp.broadcast_to(ref[r : r + 1, :], (8, 128))
+
+    entry = {(i, j): full(spread, 16 * j + i) for j in range(16) for i in range(j, 16)}
+    rows = [
+        jnp.where(lane < 16, full(lines, i), jnp.where(lane == 16 + i, 1.0, 0.0))
+        for i in range(16)
+    ]
+    for k in range(16):
+        pivot = entry[k, k]
+        inverse = 1.0 / pivot
+        for i in range(k + 1, 16):
+            scale = entry[i, k] * inverse
+            for j in range(k + 1, i + 1):
+                entry[i, j] = entry[i, j] - scale * entry[j, k]
+            rows[i] = rows[i] - scale * rows[k]
+        root = lax.rsqrt(pivot)
+        root = root * (1.5 - 0.5 * pivot * root * root)
+        lines[k : k + 1, :] = (rows[k] * root)[0:1]
+    return lines[...]
 
 
 def kernel(
@@ -148,57 +162,74 @@
     x_hbm, basis_hbm, mat_hbm, k0_hbm, ke_hbm, diag_hbm, mass_hbm, vel_hbm, shift_hbm, sample,
     total, data_hbm,
     k0, ke, diag, mass, velocities, shifts,
-    mat, xs, xh, yh, raw, applied, fields, data, full, packed, part, zpart, zsum, total_z,
-    local_sems, b_send, b_recv, x_send, x_recv, y_send, y_recv, r_send, r_recv, o_sems,
+    mat, xs, xh, yh, whole, raw, applied, fields, data, full, packed, part, zpart, zsum, total_z,
+    local_sems, b_send, b_recv, x_send, x_recv, y_send, y_recv, r_send, r_recv, o_sems, ready,
 ):
     space, sides, plane, row_count = sizes
     depth = space // plane
-    members = sides * plane
+    lines = plane // 2
+    members = sides * 2
     share = 32 // members
-    lines = plane // 2
     s = lax.axis_index("space")
     b = lax.axis_index("basis")
     z = s // plane
     spot = s - z * plane
     x = spot // 2
     core = spot - 2 * x
-    me = b * plane + spot
+    me = b * 2 + core
+    place = z * lines + x
+    holder = z < HOLDERS
+    turn = depth // 2 + 1
+    served = jnp.where(z < turn, 1, 0)
+    clients = [range(turn, depth), range(HOLDERS, turn)]
 
     def members_each(act):
-        sites = [(dx, dy) for dx in range(lines) for dy in range(sides)]
-        sites.sort(key=lambda d: -(min(d[0], lines - d[0]) + min(d[1], sides - d[1])))
-        for dx, dy in sites:
-            column, side = lax.rem(x + dx, lines), lax.rem(b + dy, sides)
-            for other in ((1 - core, core) if dx or dy else (1 - core,)):
-                index = side * plane + column * 2 + other
-                act(index, (z * plane + column * 2 + other, side))
-
-    def levels_each(act):
-        far = depth // 2
-        act((lax.rem(z + far, depth) * plane + spot, b))
-        for d in range(far - 1, 0, -1):
-            act((lax.rem(z + d, depth) * plane + spot, b))
-            act((lax.rem(z + depth - d, depth) * plane + spot, b))
+        sites = sorted(range(sides), key=lambda d: -min(d, sides - d))
+        for dy in sites:
+            side = lax.rem(b + dy, sides)
+            for other in ((1 - core, core) if dy else (1 - core,)):
+                act(side * 2 + other, (z * plane + x * 2 + other, side))
+
+    def spot_at(level, column):
+        return level * plane + column * 2 + core, b
+
+    def holders_each(act):
+        for level in range(HOLDERS):
+            for column in range(lines):
+                pl.when(place != level * lines + column)(
+                    lambda level=level, column=column: act(spot_at(level, column))
+                )
 
     barrier = pltpu.get_barrier_semaphore()
 
     def greet(peer):
         pl.semaphore_signal(barrier, inc=1, device_id=peer, device_id_type=MESH)
 
-    over = (spot == plane - 1) & (z < depth - 1)
-    under = (spot == 0) & (z > 0)
-    levels_each(greet)
-
-    @pl.when(over | under)
-    def _():
-        greet((jnp.where(over, s + 1, s - 1), b))
-
+    beside = s + 2 * core - 1
+    has_beside = (beside >= 0) & (beside < space)
     members_each(lambda index, peer: greet(peer))
+
+    @pl.when(has_beside)
+    def _():
+        greet((beside, b))
+
+    @pl.when(holder)
+    def _():
+        for level in range(HOLDERS):
+            for column in range(lines):
+                pl.when(place != level * lines + column)(
+                    lambda level=level, column=column: greet(spot_at(level, column))
+                )
+
+        @pl.loop(HOLDERS, depth)
+        def _(level):
+            for column in range(lines):
+                greet(spot_at(level, column))
 
     small = [
         (vel_hbm, velocities), (shift_hbm, shifts), (k0_hbm, k0),
         (ke_hbm, ke), (diag_hbm, diag), (mass_hbm, mass), (mat_hbm, mat),
-        (x_hbm.at[:, :, 0], xs),
+        (basis_hbm.at[:, :, 0], whole), (x_hbm.at[:, :, 0], xs),
         (basis_hbm.at[:, :, 0, pl.ds(pl.multiple_of(b * 8, 8), 8), :], raw.at[b]),
     ]
     small = [
@@ -208,8 +239,15 @@
     for copy in small:
         copy.start()
 
-    extra = jnp.where(over | under, 1, 0)
-    pl.semaphore_wait(barrier, members + depth - 2 + extra)
+    known = members - 1 + HOLDERS * lines
+    known = known + jnp.where(has_beside, 1, 0) - jnp.where(holder, 1, 0)
+    pl.semaphore_wait(barrier, known)
+
+    @pl.when(jnp.logical_not(holder))
+    def _():
+        pl.semaphore_signal(
+            ready, inc=1, device_id=spot_at(served, x), device_id_type=MESH
+        )
 
     def remote(source, target, send, recv, peer):
         return pltpu.make_async_remote_copy(
@@ -220,7 +258,7 @@
     def basis_copy(k, c):
         side = lax.rem(b + k, sides)
         return remote(
-            basis_hbm.at[:, c, 0, pl.ds(pl.multiple_of(side * 8, 8), 8), :],
+            whole.at[:, c, pl.ds(pl.multiple_of(side * 8, 8), 8), :],
             raw.at[b, :, c], b_send.at[k - 1, c], b_recv.at[k - 1, c], (s, side),
         )
 
@@ -242,6 +280,7 @@
     y_gets = [b > 0, b < sides - 1]
     for way in range(2):
         pl.when(y_sends[way])(lambda way=way: y_copy(way).start())
+    small[7].wait()
     for c in range(3):
         for k in (2, 1, 3):
             basis_copy(k, c).start()
@@ -251,11 +290,11 @@
     for copy in small[:7]:
         copy.wait()
     fill_fields(mat, k0, ke, diag, mass, velocities, shifts, sample, fields)
-    small[8].wait()
+    small[9].wait()
     own = pl.multiple_of(b * 16, 16)
     for c in range(3):
         split_rows(raw.at[b].reshape(384, 128), data, own, c)
-    small[7].wait()
+    small[8].wait()
 
     for way in range(2):
         @pl.when(jnp.logical_not(x_gets[way]))
@@ -288,9 +327,6 @@
     full[:, 0:80] = products[:, 0:80] + products[:, 80:160]
     pack_upper(full, packed)
 
-    data_out = pltpu.make_async_copy(data, data_hbm, o_sems.at[0])
-    data_out.start()
-
     def rows_of(index):
         return pl.ds(index * share, share)
 
@@ -299,18 +335,24 @@
             packed.at[rows_of(index)], part.at[rows_of(me)], r_send.at[0], r_recv.at[0], peer
         ).start()
 
-    def along(peer):
-        remote(zpart, zsum.at[rows_of(z)], r_send.at[1], r_recv.at[1], peer).start()
+    def to_holder(peer):
+        remote(zpart, zsum.at[rows_of(place)], r_send.at[1], r_recv.at[1], peer).start()
+
+    def to_client(level):
+        remote(total_z, total_z, r_send.at[3], r_recv.at[3], spot_at(level, x)).start()
 
     def gather(index, peer):
         remote(total_z, total.at[rows_of(me)], r_send.at[2], r_recv.at[2], peer).start()
 
     def fold(ref, count):
-        if share == 1:
-            return jnp.sum(ref[...], axis=0, keepdims=True)
-        return functools.reduce(
-            lambda a, c: a + c, [ref[m * share : (m + 1) * share] for m in range(count)]
-        )
+        tiles = [ref[8 * i : 8 * i + 8] for i in range(count * share // 8)]
+        while len(tiles) > 1:
+            half = (len(tiles) + 1) // 2
+            tiles = [
+                tiles[i] + tiles[i + half] if i + half < len(tiles) else tiles[i]
+                for i in range(half)
+            ]
+        return tiles[0][0:4] + tiles[0][4:8]
 
     def wait_rows(ref, count, sem):
         view = ref.at[pl.ds(0, count * share)]
@@ -318,12 +360,29 @@
 
     members_each(scatter)
     part[rows_of(me)] = packed[rows_of(me)]
+    data_out = pltpu.make_async_copy(data, data_hbm, o_sems.at[0])
+    data_out.start()
     wait_rows(part, members - 1, r_recv.at[0])
     zpart[...] = fold(part, members)
-    levels_each(along)
-    zsum[rows_of(z)] = zpart[...]
-    wait_rows(zsum, depth - 1, r_recv.at[1])
-    total_z[...] = fold(zsum, depth)
+    holders_each(to_holder)
+
+    @pl.when(holder)
+    def _():
+        zsum[rows_of(place)] = zpart[...]
+        wait_rows(zsum, depth * lines - 1, r_recv.at[1])
+        total_z[...] = fold(zsum, depth * lines)
+
+    for level in range(HOLDERS):
+        @pl.when(z == level)
+        def _():
+            pl.semaphore_wait(ready, len(clients[level]))
+            for client in clients[level]:
+                to_client(client)
+
+    @pl.when(jnp.logical_not(holder))
+    def _():
+        wait_rows(total_z, 1, r_recv.at[3])
+
     members_each(gather)
     own_rows = pltpu.make_async_copy(total_z, total.at[rows_of(me)], o_sems.at[1])
     own_rows.start()
@@ -337,14 +396,27 @@
         pl.when(x_sends[way])(lambda way=way: x_copy(way).wait_send())
         pl.when(y_sends[way])(lambda way=way: y_copy(way).wait_send())
     wait_rows(part, members - 1, r_send.at[0])
-    wait_rows(zsum, depth - 1, r_send.at[1])
+
+    @pl.when(holder)
+    def _():
+        wait_rows(zsum, HOLDERS * lines - 1, r_send.at[1])
+
+    @pl.when(jnp.logical_not(holder))
+    def _():
+        wait_rows(zsum, HOLDERS * lines, r_send.at[1])
+
+    for level in range(HOLDERS):
+        @pl.when(z == level)
+        def _():
+            wait_rows(zsum, len(clients[level]), r_send.at[3])
+
     wait_rows(total, members - 1, r_send.at[2])
 
 
 def finish(
     row_count,
     total_hbm, data_hbm, ortho_hbm, coeff_hbm, upper_hbm,
-    total, data, full, weights, result, coeff, upper, i_sems, o_sems,
+    total, data, full, weights, result, coeff, upper, spread, lines, i_sems, o_sems,
 ):
     total_in = pltpu.make_async_copy(total_hbm, total, i_sems.at[0])
     total_in.start()
@@ -368,7 +440,7 @@
     image = dot_exact(moments, mix)
     mix_t = mix.T[0:16]
     gram = dot_exact(mix_t, image)
-    factors = factor(gram)
+    factors = factor(gram, spread, lines)
     upper[...] = jnp.where(iota((16, 16), 0) <= iota((16, 16), 1), factors[:, 0:16], 0.0)
     upper_out = pltpu.make_async_copy(upper, upper_hbm, o_sems.at[1])
     upper_out.start()
@@ -384,21 +456,28 @@
     data_in.wait()
     left = weights[:, 0:160].astype(BF16)
     out = result.reshape(384, 128)
-    for t in range(0, 24, 2):
-        piece = jnp.dot(left, data[:, t * 128 : t * 128 + 256], preferred_element_type=F32)
-        piece = piece[0:16] + piece[16:32]
-        out[pl.ds(t, 16, stride=24), :] = piece[:, 0:128]
-        out[pl.ds(t + 1, 16, stride=24), :] = piece[:, 128:256]
-    ortho_out = pltpu.make_async_copy(result, ortho_hbm.at[:, :, 0], o_sems.at[2])
-    ortho_out.start()
+    ortho_out = []
+    for c in range(3):
+        for t in range(8 * c, 8 * c + 8, 2):
+            piece = jnp.dot(
+                left, data[:, t * 128 : t * 128 + 256], preferred_element_type=F32
+            )
+            piece = piece[0:16] + piece[16:32]
+            out[pl.ds(t, 16, stride=24), :] = piece[:, 0:128]
+            out[pl.ds(t + 1, 16, stride=24), :] = piece[:, 128:256]
+        ortho_out.append(
+            pltpu.make_async_copy(result.at[:, c], ortho_hbm.at[:, c, 0], o_sems.at[2 + c])
+        )
+        ortho_out[c].start()
     coeff_out.wait()
     upper_out.wait()
-    ortho_out.wait()
+    for copy in ortho_out:
+        copy.wait()
 
 
 def shards(space, sides, x_block, basis, material, k0, diag, ke, mass, velocities, shifts, sample):
     plane = PLANE
-    share = 32 // (sides * plane)
+    share = 32 // (sides * 2)
     depth = space // plane
     row_count = 3.0 * space * x_block.shape[3] * sides * x_block.shape[4]
     vmem, smem, dma = pltpu.VMEM, pltpu.SMEM, pltpu.SemaphoreType.DMA
@@ -407,12 +486,13 @@
         smem((3, 3, 8, 7), F32), smem((3, 3, 8, 7), F32), smem((3, 8), F32), smem((3, 8), F32),
         smem((8, 128), F32), smem((8, 128), F32),
         vmem((1, 8, 128), jnp.int32), vmem(block, F32), vmem((2,) + block, F32),
-        vmem((2, 16, 3, 1, 128), F32), vmem((sides,) + block, F32), vmem(block, F32),
+        vmem((2, 16, 3, 1, 128), F32), vmem((16, 3, 32, 128), F32), vmem((sides,) + block, F32), vmem(block, F32),
         vmem((63, 8, 128), F32), vmem((160, 3072), BF16), vmem((80, 128), F32),
         vmem((32, 128), F32), vmem((32, 128), F32), vmem((share, 128), F32),
-        vmem((depth * share, 128), F32), vmem((share, 128), F32),
-        dma((9,)), dma((3, 3)), dma((3, 3)), dma((2,)), dma((2,)), dma((2,)), dma((2,)),
-        dma((3,)), dma((3,)), dma((2,)),
+        vmem((depth * plane // 2 * share, 128), F32), vmem((share, 128), F32),
+        dma((10,)), dma((3, 3)), dma((3, 3)), dma((2,)), dma((2,)), dma((2,)), dma((2,)),
+        dma((4,)), dma((4,)), dma((2,)),
+        pltpu.SemaphoreType.REGULAR,
     ]
     whole = pl.BlockSpec(memory_space=pltpu.HBM)
     outs = pl.pallas_call(
@@ -444,7 +524,7 @@
         scratch_shapes=[
             vmem((32, 128), F32), vmem((160, 3072), BF16), vmem((80, 128), F32),
             vmem((32, 256), F32), vmem(block, F32), vmem((16, 16), F32), vmem((16, 16), F32),
-            dma((2,)), dma((3,)),
+            vmem((256, 128), F32), vmem((16, 128), F32), dma((2,)), dma((5,)),
         ],
         compiler_params=pltpu.CompilerParams(vmem_limit_bytes=64 * 1024 * 1024),
     )(*outs)

time: 50.1 us -> 46.4 us (0.926)
  Pallas kernels: 48.6 us -> 44.9 us
    pallas_call x1, Pallas kernels: 44.1 us -> 41.7 us  [shards(): pl.pallas_call(functools.partial(kernel, (space, sides, plane, row_count)...]
    pallas_call x1, Pallas kernels: 4.56 us -> 3.18 us  [shards(): pl.pallas_call(functools.partial(finish, row_count), out_shape=(jax.Shape...]
where the time goes in v3:
time: 46.4 us; the launch traced here: 46.2 us
  Pallas kernels  44.9 us (97%)
  between operations  1.29 us (3%)
    pallas_call x1, Pallas kernels, shards(): pl.pallas_call(functools.partial(kernel, (space, sides, plane, row_count)...  41.7 us
    pallas_call x1, Pallas kernels, shards(): pl.pallas_call(functools.partial(finish, row_count), out_shape=(jax.Shape...  3.18 us

profile of v3, /device:TPU:1, one launch (start us, length us, event | category | flops | bytes accessed | tf_op | source)
XLA Modules:
  0.0 46.2 jit_solution(13651847350226633355)
XLA Ops:
  1.3 41.7 %shard_map.121 = (f32[32,128]{1,0:T(8,128)}, bf16[160,3072]{1,0:T(8,128)(2,1)}) custom-call(f32[16,3,1,8,128]{4,3,2,1,0:T(8,128)} %x_hbm.1, f32[16,3,1,32,128]{4,3,2,1,0:T(8,128)} %basis_hbm.1, s32[1,8,128]{2,1,0:T(8,128)} %mat_hbm.1, f32[3,3,8,7]{3,2,1,0:T(8,128)} %bitcast.6, f32[3,3,8,7]{3,2,1,0:T(8,128)} %bitcast.7, f32[3,8]{1,0:T(4,128)} %bitcast.10, ...), custom_call_target="tpu_custom_call" | custom-call | tf_op jit(solution)/shard_map/pallas_call | solution.py:498
  43.0 3.2 %shard_map.122 = (f32[16,3,1,8,128]{4,3,2,1,0:T(8,128)}, f32[16,16]{1,0:T(8,128)}, f32[16,16]{1,0:T(8,128)}) custom-call(f32[32,128]{1,0:T(8,128)} %get-tuple-element.5.total_hbm, bf16[160,3072]{1,0:T(8,128)(2,1)} %get-tuple-element.6.data_hbm), custom_call_target="tpu_custom_call" | custom-call | tf_op jit(solution)/shard_map/pallas_call | solution.py:515

commit v4 on v3

--- a/solution.py
+++ b/solution.py
@@ -9,7 +9,7 @@
 
 MESH = pl.DeviceIdType.MESH
 PLANE = 8
-HOLDERS = 2
+HOLDERS = 4
 EXACT = lax.Precision.HIGHEST
 F32 = jnp.float32
 BF16 = jnp.bfloat16
@@ -179,9 +179,9 @@
     me = b * 2 + core
     place = z * lines + x
     holder = z < HOLDERS
-    turn = depth // 2 + 1
-    served = jnp.where(z < turn, 1, 0)
-    clients = [range(turn, depth), range(HOLDERS, turn)]
+    turn = (depth + HOLDERS) // 2
+    served = jnp.where(z < turn, HOLDERS - 1, 0)
+    clients = {0: range(turn, depth), HOLDERS - 1: range(HOLDERS, turn)}
 
     def members_each(act):
         sites = sorted(range(sides), key=lambda d: -min(d, sides - d))
@@ -207,11 +207,11 @@
 
     beside = s + 2 * core - 1
     has_beside = (beside >= 0) & (beside < space)
+    @pl.when(has_beside)
+    def _():
+        greet((beside, b))
+
     members_each(lambda index, peer: greet(peer))
-
-    @pl.when(has_beside)
-    def _():
-        greet((beside, b))
 
     @pl.when(holder)
     def _():
@@ -371,8 +371,9 @@
         zsum[rows_of(place)] = zpart[...]
         wait_rows(zsum, depth * lines - 1, r_recv.at[1])
         total_z[...] = fold(zsum, depth * lines)
-
-    for level in range(HOLDERS):
+        members_each(gather)
+
+    for level in clients:
         @pl.when(z == level)
         def _():
             pl.semaphore_wait(ready, len(clients[level]))
@@ -382,12 +383,10 @@
     @pl.when(jnp.logical_not(holder))
     def _():
         wait_rows(total_z, 1, r_recv.at[3])
-
-    members_each(gather)
+        members_each(gather)
+
     own_rows = pltpu.make_async_copy(total_z, total.at[rows_of(me)], o_sems.at[1])
     own_rows.start()
-    wait_rows(total, members - 1, r_recv.at[2])
-    own_rows.wait()
     data_out.wait()
     for c in range(3):
         for k in (1, 2, 3):
@@ -405,11 +404,13 @@
     def _():
         wait_rows(zsum, HOLDERS * lines, r_send.at[1])
 
-    for level in range(HOLDERS):
+    for level in clients:
         @pl.when(z == level)
         def _():
             wait_rows(zsum, len(clients[level]), r_send.at[3])
 
+    wait_rows(total, members - 1, r_recv.at[2])
+    own_rows.wait()
     wait_rows(total, members - 1, r_send.at[2])
 
 

time: 46.4 us -> 46.3 us (level)
  no operation moved by 1% of the time
where the time goes in v4:
time: 46.3 us; the launch traced here: 46.1 us
  Pallas kernels  44.8 us (97%)
  between operations  1.29 us (3%)
    pallas_call x1, Pallas kernels, shards(): pl.pallas_call(functools.partial(kernel, (space, sides, plane, row_count)...  41.6 us
    pallas_call x1, Pallas kernels, shards(): pl.pallas_call(functools.partial(finish, row_count), out_shape=(jax.Shape...  3.17 us

profile of v4, /device:TPU:1, one launch (start us, length us, event | category | flops | bytes accessed | tf_op | source)
XLA Modules:
  0.0 46.1 jit_solution(563066668275944824)
XLA Ops:
  1.3 41.6 %shard_map.121 = (f32[32,128]{1,0:T(8,128)}, bf16[160,3072]{1,0:T(8,128)(2,1)}) custom-call(f32[16,3,1,8,128]{4,3,2,1,0:T(8,128)} %x_hbm.1, f32[16,3,1,32,128]{4,3,2,1,0:T(8,128)} %basis_hbm.1, s32[1,8,128]{2,1,0:T(8,128)} %mat_hbm.1, f32[3,3,8,7]{3,2,1,0:T(8,128)} %bitcast.6, f32[3,3,8,7]{3,2,1,0:T(8,128)} %bitcast.7, f32[3,8]{1,0:T(4,128)} %bitcast.10, ...), custom_call_target="tpu_custom_call" | custom-call | tf_op jit(solution)/shard_map/pallas_call | solution.py:499
  42.9 3.2 %shard_map.122 = (f32[16,3,1,8,128]{4,3,2,1,0:T(8,128)}, f32[16,16]{1,0:T(8,128)}, f32[16,16]{1,0:T(8,128)}) custom-call(f32[32,128]{1,0:T(8,128)} %get-tuple-element.5.total_hbm, bf16[160,3072]{1,0:T(8,128)(2,1)} %get-tuple-element.6.data_hbm), custom_call_target="tpu_custom_call" | custom-call | tf_op jit(solution)/shard_map/pallas_call | solution.py:516

commit v5 on v4

--- a/solution.py
+++ b/solution.py
@@ -278,12 +278,13 @@
     x_gets = [s > 0, s < space - 1]
     y_sends = [b < sides - 1, b > 0]
     y_gets = [b > 0, b < sides - 1]
-    for way in range(2):
-        pl.when(y_sends[way])(lambda way=way: y_copy(way).start())
     small[7].wait()
     for c in range(3):
         for k in (2, 1, 3):
             basis_copy(k, c).start()
+        if c == 0:
+            for way in range(2):
+                pl.when(y_sends[way])(lambda way=way: y_copy(way).start())
     for way in range(2):
         pl.when(x_sends[way])(lambda way=way: x_copy(way).start())
 

time: 46.3 us -> 46.1 us (level)
  no operation moved by 1% of the time
where the time goes in v5:
time: 46.1 us; the launch traced here: 45.9 us
  Pallas kernels  44.6 us (97%)
  between operations  1.29 us (3%)
    pallas_call x1, Pallas kernels, shards(): pl.pallas_call(functools.partial(kernel, (space, sides, plane, row_count)...  41.4 us
    pallas_call x1, Pallas kernels, shards(): pl.pallas_call(functools.partial(finish, row_count), out_shape=(jax.Shape...  3.18 us

profile of v5, /device:TPU:1, one launch (start us, length us, event | category | flops | bytes accessed | tf_op | source)
XLA Modules:
  0.0 45.9 jit_solution(16733259912822839653)
XLA Ops:
  1.3 41.4 %shard_map.121 = (f32[32,128]{1,0:T(8,128)}, bf16[160,3072]{1,0:T(8,128)(2,1)}) custom-call(f32[16,3,1,8,128]{4,3,2,1,0:T(8,128)} %x_hbm.1, f32[16,3,1,32,128]{4,3,2,1,0:T(8,128)} %basis_hbm.1, s32[1,8,128]{2,1,0:T(8,128)} %mat_hbm.1, f32[3,3,8,7]{3,2,1,0:T(8,128)} %bitcast.6, f32[3,3,8,7]{3,2,1,0:T(8,128)} %bitcast.7, f32[3,8]{1,0:T(4,128)} %bitcast.10, ...), custom_call_target="tpu_custom_call" | custom-call | tf_op jit(solution)/shard_map/pallas_call | solution.py:500
  42.7 3.2 %shard_map.122 = (f32[16,3,1,8,128]{4,3,2,1,0:T(8,128)}, f32[16,16]{1,0:T(8,128)}, f32[16,16]{1,0:T(8,128)}) custom-call(f32[32,128]{1,0:T(8,128)} %get-tuple-element.5.total_hbm, bf16[160,3072]{1,0:T(8,128)(2,1)} %get-tuple-element.6.data_hbm), custom_call_target="tpu_custom_call" | custom-call | tf_op jit(solution)/shard_map/pallas_call | solution.py:517

commit v6 on v5

--- a/solution.py
+++ b/solution.py
@@ -282,7 +282,7 @@
     for c in range(3):
         for k in (2, 1, 3):
             basis_copy(k, c).start()
-        if c == 0:
+        if c == 1:
             for way in range(2):
                 pl.when(y_sends[way])(lambda way=way: y_copy(way).start())
     for way in range(2):

time: 46.1 us -> 46.1 us (level)
  no operation moved by 1% of the time
where the time goes in v6:
time: 46.1 us; the launch traced here: 45.9 us
  Pallas kernels  44.6 us (97%)
  between operations  1.29 us (3%)
    pallas_call x1, Pallas kernels, shards(): pl.pallas_call(functools.partial(kernel, (space, sides, plane, row_count)...  41.4 us
    pallas_call x1, Pallas kernels, shards(): pl.pallas_call(functools.partial(finish, row_count), out_shape=(jax.Shape...  3.18 us

profile of v6, /device:TPU:1, one launch (start us, length us, event | category | flops | bytes accessed | tf_op | source)
XLA Modules:
  0.0 45.9 jit_solution(17816870455050719145)
XLA Ops:
  1.3 41.4 %shard_map.121 = (f32[32,128]{1,0:T(8,128)}, bf16[160,3072]{1,0:T(8,128)(2,1)}) custom-call(f32[16,3,1,8,128]{4,3,2,1,0:T(8,128)} %x_hbm.1, f32[16,3,1,32,128]{4,3,2,1,0:T(8,128)} %basis_hbm.1, s32[1,8,128]{2,1,0:T(8,128)} %mat_hbm.1, f32[3,3,8,7]{3,2,1,0:T(8,128)} %bitcast.6, f32[3,3,8,7]{3,2,1,0:T(8,128)} %bitcast.7, f32[3,8]{1,0:T(4,128)} %bitcast.10, ...), custom_call_target="tpu_custom_call" | custom-call | tf_op jit(solution)/shard_map/pallas_call | solution.py:500
  42.7 3.2 %shard_map.122 = (f32[16,3,1,8,128]{4,3,2,1,0:T(8,128)}, f32[16,16]{1,0:T(8,128)}, f32[16,16]{1,0:T(8,128)}) custom-call(f32[32,128]{1,0:T(8,128)} %get-tuple-element.5.total_hbm, bf16[160,3072]{1,0:T(8,128)(2,1)} %get-tuple-element.6.data_hbm), custom_call_target="tpu_custom_call" | custom-call | tf_op jit(solution)/shard_map/pallas_call | solution.py:517
